TPU v7x, 32 devices: a whole 2x2x4 slice. The times are simulated.
32 devices in a mesh: grp: 2 (over x), seq: 16 (over z, y, core).
Axes of the slice: x: 2, y: 2, z: 4, core: 2. Of those that a mesh axis runs over, the one named last changes fastest.
Arguments:
- fast_state: bfloat16 [32, 3, 1024, 512], P(('grp', 'seq')), parts along dimension 0, may hold values from -0.25 to 0.25
- initial_fast: bfloat16 [3, 1024, 512], P(None, 'seq'), may hold values from -0.25 to 0.25
- queries: bfloat16 [32, 4, 384, 512], P(('grp', 'seq')), parts along dimension 0, may hold values from -6 to 6
- token_keys: bfloat16 [32, 4, 384, 512], P(('grp', 'seq')), parts along dimension 0, may hold values from -6 to 6
- token_values: bfloat16 [32, 4, 384, 512], P(('grp', 'seq')), parts along dimension 0, may hold values from -6 to 6
- step_sizes: bfloat16 [32, 4, 384], P(('grp', 'seq')), parts along dimension 0, may hold values from 0.0019989014 to 0.019897461
Outputs:
- layer_output: bfloat16 [32, 4, 384, 512], P(('grp', 'seq')), parts along dimension 0
There are 2 independent parts, one for each index of `grp`. A program takes and returns all parts, laid end to end along the dimension named above; an argument that names none is the same for every part. Nothing has to cross between parts.
All inputs are finite; a program needn't handle non-finite values.
Results may differ from a plain program's by a relative error of at most 0.012.
The roundings to bfloat16 on the way count: a program that leaves them out, or rounds other values in their place, can miss the bound.
Values may be sent and summed in bfloat16 or wider, within the bound.
A program may use at most 64 MiB of HBM per device.

v0:
```python
import jax
import jax.numpy as jnp
from jax import lax
from jax.sharding import PartitionSpec as P

TICKS = 4


epsilon = 1e-06


def shifted(value, axis, steps):
    count = lax.axis_size(axis)
    pairs = [(source, (source + steps) % count) for source in range(count)]
    return lax.ppermute(value, axis, pairs)


def contract_last(left_side, right_side):
    return lax.dot_general(
        left_side, right_side, (((1,), (1,)), ((), ())), preferred_element_type=jnp.float32
    )


def contract_first(left_side, right_side):
    return lax.dot_general(
        left_side, right_side, (((0,), (0,)), ((), ())), preferred_element_type=jnp.float32
    )


def rescale(updated, previous):
    old_norm = jnp.sqrt(jnp.sum(previous * previous, axis=-1, keepdims=True) + epsilon)
    new_norm = jnp.sqrt(jnp.sum(updated * updated, axis=-1, keepdims=True) + epsilon)
    return updated * (old_norm / new_norm)


def advance(fast, token_keys, token_values, step_sizes):
    gate_pre = contract_last(token_keys, fast[0])
    up_pre = contract_last(token_keys, fast[1])
    gate_sig = jax.nn.sigmoid(gate_pre)
    hidden = (gate_pre * gate_sig * up_pre).astype(jnp.bfloat16)
    target = (step_sizes.astype(jnp.float32)[:, None] * token_values.astype(jnp.float32)).astype(
        jnp.bfloat16
    )
    back_grad = contract_last(target, fast[2])
    grad_gate = (back_grad * up_pre * gate_sig * (1.0 + gate_pre * (1.0 - gate_sig))).astype(
        jnp.bfloat16
    )
    grad_up = (back_grad * gate_pre * gate_sig).astype(jnp.bfloat16)
    delta_gate = contract_first(grad_gate, token_keys)
    delta_up = contract_first(grad_up, token_keys)
    delta_down = contract_first(hidden, target)
    previous = fast.astype(jnp.float32)
    updated = previous + jnp.stack([delta_gate, delta_up, delta_down])
    return rescale(updated, previous).astype(jnp.bfloat16)


def serve_queries(fast, queries):
    gate_pre = contract_last(queries, fast[0])
    up_pre = contract_last(queries, fast[1])
    hidden = (gate_pre * jax.nn.sigmoid(gate_pre) * up_pre).astype(jnp.bfloat16)
    return jnp.dot(hidden, fast[2], preferred_element_type=jnp.float32).astype(jnp.bfloat16)


def body(fast_state, initial_fast, queries, token_keys, token_values, step_sizes):
    carried = fast_state[0]
    whole_initial = lax.all_gather(initial_fast, "seq", axis=1, tiled=True)
    position = lax.axis_index("seq")
    results = []
    section_count = lax.axis_size("seq")
    advanced = carried
    for step_index in range(TICKS):
        if step_index == 0:
            tick_queries = queries[0, 0]
            tick_keys = token_keys[0, 0]
            tick_values = token_values[0, 0]
            tick_steps = step_sizes[0, 0]
        else:
            tick_queries, tick_keys, tick_values, tick_steps = shifted(
                (
                    queries[0, step_index],
                    token_keys[0, step_index],
                    token_values[0, step_index],
                    step_sizes[0, step_index],
                ),
                "seq",
                -step_index,
            )
            restart = position + step_index == section_count
            carried = jnp.where(restart, whole_initial, advanced)
        advanced = advance(carried, tick_keys, tick_values, tick_steps)
        answer = serve_queries(advanced, tick_queries)
        if step_index == 0:
            results.append(answer)
        else:
            results.append(shifted(answer, "seq", step_index))
    return jnp.stack(results, axis=0)[None]


def solution(mesh):
    return jax.shard_map(
        body,
        mesh=mesh,
        in_specs=(
            P(("grp", "seq"), None, None, None),
            P(None, "seq", None),
            P(("grp", "seq"), None, None, None),
            P(("grp", "seq"), None, None, None),
            P(("grp", "seq"), None, None, None),
            P(("grp", "seq"), None, None),
        ),
        out_specs=P(("grp", "seq"), None, None, None),
        check_vma=False,
    )
```

profile of v0, /device:TPU:1, one launch (start us, length us, event | category | flops | bytes accessed | tf_op | source)
XLA Modules:
  0.0 195.3 jit_solution(10988839707194773126)
XLA Ops:
  8.1 5.7 %collective-permute-start.10 = (bf16[384]{0:T(512)(128)(2,1)S(1)}, bf16[384]{0:T(512)(128)(2,1)S(1)}, u32[]{:S(2)}, u32[]{:S(2)}) collective-permute-start(bf16[384]{0:T(512)(128)(2,1)S(1)} %get-tuple-element.13), channel_id=1, source_target_pairs={{0,13},{1,14},{2,15},{3,0},{4,1},{5,2},{6,3},{7,4},{8,5},{9,6},{10... | collective-permute-start | bytes 2312 | tf_op jit(solution)/shard_map/ppermute | solution.py:15
  14.1 2.3 %slice_bitcast_fusion.53 = (bf16[384,512]{1,0:T(8,128)(2,1)}, bf16[384,512]{1,0:T(8,128)(2,1)}, bf16[384,512]{1,0:T(8,128)(2,1)}) fusion(bf16[1,4,384,512]{3,2,1,0:T(8,128)(2,1)} %param.8), kind=kLoop, calls=%fused_computation.197 | loop fusion | bytes 2359296 | tf_op jit(solution)/shard_map/squeeze | solution.py:80
  16.3 1.8 collective-permute-start.3
  18.2 3.2 %copy.19 = bf16[1,3,1024,512]{2,3,1,0:T(8,128)(2,1)S(1)} copy(bf16[1,3,1024,512]{3,2,1,0:T(8,128)(2,1)} %param.6) | data formatting | bytes 6291456 | tf_op args[0]
  21.5 3.4 %slice_bitcast_fusion.49 = (bf16[384,512]{1,0:T(8,128)(2,1)}, bf16[384,512]{1,0:T(8,128)(2,1)}, bf16[384,512]{1,0:T(8,128)(2,1)}) fusion(bf16[1,4,384,512]{3,2,1,0:T(8,128)(2,1)} %param.10), kind=kLoop, calls=%fused_computation.193 | loop fusion | bytes 2359296 | tf_op jit(solution)/shard_map/squeeze | solution.py:82
  24.9 1.1 slice_bitcast_fusion.48
  28.6 0.9 convolution_bitcast_fusion.10
  29.5 1.0 convolution_bitcast_fusion.9
  30.5 1.1 convolution_bitcast_fusion.11
  31.8 1.5 fusion.3
  33.3 1.2 collective-permute-start.8
  37.1 1.3 convert_element_type.168
  38.3 46.0 %all-gather.2.cloned.1.call-done = bf16[3,1024,512]{2,1,0:T(8,128)(2,1)} async-done(((bf16[3,64,512]{2,1,0:T(8,128)(2,1)}), bf16[3,1024,512]{2,1,0:T(8,128)(2,1)}) %all-gather.2.cloned.1.call-update) | async-done | bytes 3145744 | tf_op jit(solution)/shard_map/all_gather | solution.py:66
  84.3 3.2 %copy.21 = bf16[3,1024,512]{1,2,0:T(8,128)(2,1)S(1)} copy(bf16[3,1024,512]{2,1,0:T(8,128)(2,1)} %all-gather.2.cloned.1.call-done) | data formatting | bytes 6291456 | tf_op jit(solution)/shard_map/all_gather | solution.py:66
  87.5 6.0 %broadcast_select_fusion.2 = (bf16[3,1024,512]{1,2,0:T(8,128)(2,1)S(1)}, bf16[3,1024,512]{1,2,0:T(8,128)(2,1)}) fusion(bf16[3,1024,512]{1,2,0:T(8,128)(2,1)S(1)} %copy.21, pred[]{:T(512)S(6)} %eq.9, f32[3,1024]{1,0:T(4,128)S(1)} %rsqrt_multiply_fusion.3, f32[1,1024,512]{1,2,0:T(8,128)} %copy-done.5, f32[1,1024,512]{1,2,0:T(8,128)} %copy-done.4, ...), kind=kLoop, calls=%fused_computation.22 | loop fusion | flops 11010048 | bytes 18886656 | tf_op jit(solution)/shard_map/jit(_where)/select_n | solution.py:89
  95.0 5.7 %collective-permute-done.1 = bf16[384,512]{1,0:T(8,128)(2,1)S(1)} collective-permute-done((bf16[384,512]{1,0:T(8,128)(2,1)S(1)}, bf16[384,512]{1,0:T(8,128)(2,1)S(1)}, u32[]{:S(2)}, u32[]{:S(2)}) %collective-permute-start.1) | collective-permute-done | bytes 393248 | tf_op jit(solution)/shard_map/ppermute | solution.py:15
  100.8 4.5 %collective-permute-start.6 = (bf16[384,512]{1,0:T(8,128)(2,1)}, bf16[384,512]{1,0:T(8,128)(2,1)}, u32[]{:S(2)}, u32[]{:S(2)}) collective-permute-start(bf16[384,512]{1,0:T(8,128)(2,1)} %get-tuple-element.27), channel_id=1, source_target_pairs={{0,14},{1,15},{2,0},{3,1},{4,2},{5,3},{6,4},{7,5},{8,6},{9,7},{10,... | collective-permute-start | bytes 1179656 | tf_op jit(solution)/shard_map/ppermute | solution.py:15
  105.9 0.9 convolution_bitcast_fusion.6
  106.9 1.0 convolution_bitcast_fusion.8
  107.9 0.9 convolution_bitcast_fusion.7
  108.8 1.4 fusion
  110.3 3.6 %broadcast_select_fusion.1 = (bf16[3,1024,512]{1,2,0:T(8,128)(2,1)}, bf16[3,1024,512]{1,2,0:T(8,128)(2,1)S(1)}) fusion(bf16[3,1024,512]{1,2,0:T(8,128)(2,1)S(1)} %copy.21, pred[]{:T(512)S(6)} %eq.10, f32[3,1024]{1,0:T(4,128)S(1)} %rsqrt_multiply_fusion.2, f32[1,1024,512]{1,2,0:T(8,128)S(1)} %convolution_bitcast_fusion.6, ...), kind=kLoop, calls=%fused_computation.21 | loop fusion | flops 11010048 | bytes 18886656 | tf_op jit(solution)/shard_map/jit(_where)/select_n | solution.py:89
  113.9 1.7 copy-done.8
  115.6 2.7 %fusion.62 = f32[1024,384]{0,1:T(8,128)} fusion(bf16[384,512]{1,0:T(8,128)(2,1)} %collective-permute-done.3, bf16[3,1024,512]{1,2,0:T(8,128)(2,1)S(1)} %get-tuple-element.19), kind=kOutput, calls=%fused_computation.144 | convolution fusion | flops 402653184 | bytes 3014656 | tf_op jit(solution)/shard_map/dot_general | solution.py:19
  118.4 4.0 %convolution_convert_fusion.2 = bf16[384,512]{1,0:T(8,128)(2,1)} fusion(f32[1024,384]{0,1:T(8,128)} %fusion.62, bf16[384,512]{1,0:T(8,128)(2,1)} %collective-permute-done.3, bf16[3,1024,512]{1,2,0:T(8,128)(2,1)} %copy-done.8), kind=kOutput, calls=%fused_computation.118 | convolution fusion | flops 807862272 | bytes 4456448 | tf_op jit(solution)/shard_map/dot_general | solution.py:61
  123.5 3.3 %collective-permute-start.12 = (bf16[384,512]{1,0:T(8,128)(2,1)}, bf16[384,512]{1,0:T(8,128)(2,1)S(1)}, u32[]{:S(2)}, u32[]{:S(2)}) collective-permute-start(bf16[384,512]{1,0:T(8,128)(2,1)} %get-tuple-element.28), channel_id=1, source_target_pairs={{0,13},{1,14},{2,15},{3,0},{4,1},{5,2},{6,3},{7,4},{8,5},{9,6},{10... | collective-permute-start | bytes 1179656 | tf_op jit(solution)/shard_map/ppermute | solution.py:15
  126.7 2.1 %fusion.59 = f32[1024,384]{0,1:T(8,128)S(1)} fusion(bf16[384,512]{1,0:T(8,128)(2,1)} %copy-done.13, bf16[3,1024,512]{1,2,0:T(8,128)(2,1)} %get-tuple-element.18), kind=kOutput, calls=%fused_computation.136 | convolution fusion | flops 402653184 | bytes 3014656 | tf_op jit(solution)/shard_map/dot_general | solution.py:19
  128.8 1.8 fusion.60
  130.7 1.4 collective-permute-start.4
  132.1 1.6 fusion.61
  133.7 2.0 %convolution_bitcast_fusion.3 = f32[1,1024,512]{1,2,0:T(8,128)S(1)} fusion(f32[1024,384]{0,1:T(8,128)S(1)} %fusion.59, f32[1024,384]{0,1:T(8,128)S(1)} %fusion.60, bf16[384,512]{1,0:T(8,128)(2,1)} %collective-permute-done.6, f32[384]{0:T(512)S(1)} %copy-done.18), kind=kOutput, calls=%fused_computation.26 | convolution fusion | flops 405602304 | bytes 5637632 | tf_op jit(solution)/shard_map/dot_general | solution.py:25
  135.7 1.0 convolution_bitcast_fusion.5
  137.6 1.4 fusion.1
  139.1 3.6 %broadcast_select_fusion = (bf16[3,1024,512]{1,2,0:T(8,128)(2,1)}, bf16[3,1024,512]{1,2,0:T(8,128)(2,1)S(1)}) fusion(bf16[3,1024,512]{1,2,0:T(8,128)(2,1)S(1)} %copy.21, pred[]{:T(512)S(6)} %eq.11, f32[3,1024]{1,0:T(4,128)S(1)} %rsqrt_multiply_fusion.1, f32[1,1024,512]{1,2,0:T(8,128)S(1)} %convolution_bitcast_fusion.3, ...), kind=kLoop, calls=%fused_computation.20 | loop fusion | flops 11010048 | bytes 18886656 | tf_op jit(solution)/shard_map/jit(_where)/select_n | solution.py:89
  142.7 1.7 copy-done.9
  144.4 2.7 %fusion.58 = f32[1024,384]{0,1:T(8,128)} fusion(bf16[384,512]{1,0:T(8,128)(2,1)} %collective-permute-done.8, bf16[3,1024,512]{1,2,0:T(8,128)(2,1)S(1)} %get-tuple-element.17), kind=kOutput, calls=%fused_computation.134 | convolution fusion | flops 402653184 | bytes 3014656 | tf_op jit(solution)/shard_map/dot_general | solution.py:19
  147.1 4.1 %convolution_convert_fusion.1 = bf16[384,512]{1,0:T(8,128)(2,1)} fusion(f32[1024,384]{0,1:T(8,128)} %fusion.58, bf16[384,512]{1,0:T(8,128)(2,1)} %collective-permute-done.8, bf16[3,1024,512]{1,2,0:T(8,128)(2,1)} %copy-done.9), kind=kOutput, calls=%fused_computation.117 | convolution fusion | flops 807862272 | bytes 4456448 | tf_op jit(solution)/shard_map/dot_general | solution.py:61
  152.5 1.6 fusion.57
  154.2 2.0 %convolution_bitcast_fusion = f32[1,1024,512]{1,2,0:T(8,128)S(1)} fusion(f32[1024,384]{0,1:T(8,128)S(1)} %fusion.55, f32[1024,384]{0,1:T(8,128)S(1)} %fusion.56, bf16[384,512]{1,0:T(8,128)(2,1)} %collective-permute-done.11, f32[384]{0:T(512)S(1)} %copy-done.17), kind=kOutput, calls=%fused_computation.23 | convolution fusion | flops 405602304 | bytes 5637632 | tf_op jit(solution)/shard_map/dot_general | solution.py:25
  156.1 1.0 convolution_bitcast_fusion.2
  158.1 1.5 fusion.2
  159.6 1.4 multiply_convert_fusion
  161.1 4.1 %fusion.66 = f32[1024,384]{0,1:T(8,128)} fusion(bf16[3,1024,512]{1,2,0:T(8,128)(2,1)} %get-tuple-element.21, bf16[1,4,384,512]{3,2,1,0:T(8,128)(2,1)} %param.8), kind=kOutput, calls=%fused_computation.154 | convolution fusion | flops 402653184 | bytes 3014656 | tf_op jit(solution)/shard_map/dot_general | solution.py:19
  165.2 2.7 %fusion.54 = f32[1024,384]{0,1:T(8,128)} fusion(bf16[384,512]{1,0:T(8,128)(2,1)} %collective-permute-done.13, bf16[3,1024,512]{1,2,0:T(8,128)(2,1)S(1)} %multiply_convert_fusion), kind=kOutput, calls=%fused_computation.124 | convolution fusion | flops 402653184 | bytes 3014656 | tf_op jit(solution)/shard_map/dot_general | solution.py:19
  167.9 4.2 %convolution_convert_fusion = bf16[384,512]{1,0:T(8,128)(2,1)} fusion(f32[1024,384]{0,1:T(8,128)} %fusion.54, bf16[384,512]{1,0:T(8,128)(2,1)} %collective-permute-done.13, bf16[3,1024,512]{1,2,0:T(8,128)(2,1)} %copy-done.10), kind=kOutput, calls=%fused_computation.116 | convolution fusion | flops 807862272 | bytes 4456448 | tf_op jit(solution)/shard_map/dot_general | solution.py:61
  172.1 3.5 %fusion.53 = bf16[1,384,512]{2,1,0:T(8,128)(2,1)} fusion(bf16[3,1024,512]{1,2,0:T(8,128)(2,1)S(1)} %copy-done.7, f32[1024,384]{0,1:T(8,128)} %fusion.66, bf16[1,4,384,512]{3,2,1,0:T(8,128)(2,1)} %param.8), kind=kOutput, calls=%fused_computation.120 | convolution fusion | flops 807862272 | bytes 4456448 | tf_op jit(solution)/shard_map/dot_general | solution.py:61
  175.6 10.2 %collective-permute-done.14 = bf16[384,512]{1,0:T(8,128)(2,1)S(1)} collective-permute-done((bf16[384,512]{1,0:T(8,128)(2,1)}, bf16[384,512]{1,0:T(8,128)(2,1)S(1)}, u32[]{:S(2)}, u32[]{:S(2)}) %collective-permute-start.14) | collective-permute-done | bytes 393248 | tf_op jit(solution)/shard_map/ppermute | solution.py:15
  185.9 2.6 %maximum_bitcast_fusion = bf16[1,4,384,512]{3,2,1,0:T(8,128)(2,1)} fusion(bf16[1,384,512]{2,1,0:T(8,128)(2,1)S(1)} %bitcast.391, bf16[1,384,512]{2,1,0:T(8,128)(2,1)} %bitcast.51, bf16[1,384,512]{2,1,0:T(8,128)(2,1)} %bitcast.34, bf16[1,384,512]{2,1,0:T(8,128)(2,1)} %fusion.53), kind=kLoop, calls=%fused_computation.35 | loop fusion | flops 2359296 | bytes 3145728 | tf_op jit(solution)/shard_map/broadcast_in_dim | solution.py:96
  (82 shorter events, 13.6 us)
Async XLA Ops:
  6.5 77.8 %all-gather.2.cloned.1.call-start = ((), (), s32[]{:S(2)}) async-start(), calls=%async_computation | async-start | bytes 3342336 | tf_op jit(solution)/shard_map/all_gather | solution.py:66
  8.1 25.2 %collective-permute-start.10 = (bf16[384]{0:T(512)(128)(2,1)S(1)}, bf16[384]{0:T(512)(128)(2,1)S(1)}, u32[]{:S(2)}, u32[]{:S(2)}) collective-permute-start(bf16[384]{0:T(512)(128)(2,1)S(1)} %get-tuple-element.13), channel_id=1, source_target_pairs={{0,13},{1,14},{2,15},{3,0},{4,1},{5,2},{6,3},{7,4},{8,5},{9,6},{10... | collective-permute-start | bytes 2312 | tf_op jit(solution)/shard_map/ppermute | solution.py:15
  13.8 21.3 %collective-permute-start = (bf16[384]{0:T(512)(128)(2,1)S(1)}, bf16[384]{0:T(512)(128)(2,1)S(1)}, u32[]{:S(2)}, u32[]{:S(2)}) collective-permute-start(bf16[384]{0:T(512)(128)(2,1)S(1)} %get-tuple-element.14), channel_id=1, source_target_pairs={{0,15},{1,0},{2,1},{3,2},{4,3},{5,4},{6,5},{7,6},{8,7},{9,8},{10,9... | collective-permute-start | bytes 2312 | tf_op jit(solution)/shard_map/ppermute | solution.py:15
  13.8 22.7 %collective-permute-start.5 = (bf16[384]{0:T(512)(128)(2,1)S(1)}, bf16[384]{0:T(512)(128)(2,1)S(1)}, u32[]{:S(2)}, u32[]{:S(2)}) collective-permute-start(bf16[384]{0:T(512)(128)(2,1)S(1)} %get-tuple-element.15), channel_id=1, source_target_pairs={{0,14},{1,15},{2,0},{3,1},{4,2},{5,3},{6,4},{7,5},{8,6},{9,7},{10,... | collective-permute-start | bytes 2312 | tf_op jit(solution)/shard_map/ppermute | solution.py:15
  16.3 97.6 %collective-permute-start.3 = (bf16[384,512]{1,0:T(8,128)(2,1)}, bf16[384,512]{1,0:T(8,128)(2,1)}, u32[]{:S(2)}, u32[]{:S(2)}) collective-permute-start(bf16[384,512]{1,0:T(8,128)(2,1)} %get-tuple-element.22), channel_id=1, source_target_pairs={{0,15},{1,0},{2,1},{3,2},{4,3},{5,4},{6,5},{7,6},{8,7},{9,8},{10,9... | collective-permute-start | bytes 1179656 | tf_op jit(solution)/shard_map/ppermute | solution.py:15
  18.1 3.4 %copy-start.16 = (bf16[1,4,384]{2,1,0:T(4,128)(2,1)S(1)}, bf16[1,4,384]{2,1,0:T(4,128)(2,1)}, u32[]{:S(2)}) copy-start(bf16[1,4,384]{2,1,0:T(4,128)(2,1)} %param.11) | copy-start | bytes 9220
  18.1 147.1 %collective-permute-start.13 = (bf16[384,512]{1,0:T(8,128)(2,1)}, bf16[384,512]{1,0:T(8,128)(2,1)}, u32[]{:S(2)}, u32[]{:S(2)}) collective-permute-start(bf16[384,512]{1,0:T(8,128)(2,1)} %get-tuple-element.23), channel_id=1, source_target_pairs={{0,13},{1,14},{2,15},{3,0},{4,1},{5,2},{6,3},{7,4},{8,5},{9,6},{10... | collective-permute-start | bytes 1179656 | tf_op jit(solution)/shard_map/ppermute | solution.py:15
  21.4 10.1 %copy-start.2 = (bf16[1,3,1024,512]{2,3,1,0:T(8,128)(2,1)}, bf16[1,3,1024,512]{2,3,1,0:T(8,128)(2,1)S(1)}, u32[]{:S(2)}) copy-start(bf16[1,3,1024,512]{2,3,1,0:T(8,128)(2,1)S(1)} %copy.19) | copy-start | bytes 9437188
  21.5 3.4 %copy-start.11 = (bf16[1,4,384,512]{3,2,1,0:T(8,128)(2,1)S(1)}, bf16[1,4,384,512]{3,2,1,0:T(8,128)(2,1)}, u32[]{:S(2)}) copy-start(bf16[1,4,384,512]{3,2,1,0:T(8,128)(2,1)} %param.9) | copy-start | bytes 4718596
  21.5 4.4 %copy-start.3 = (bf16[1,3,1024,512]{3,2,1,0:T(8,128)(2,1)S(1)}, bf16[1,3,1024,512]{3,2,1,0:T(8,128)(2,1)}, u32[]{:S(2)}) copy-start(bf16[1,3,1024,512]{3,2,1,0:T(8,128)(2,1)} %param.6) | copy-start | bytes 9437188
  26.5 1.4 copy-start.12
  29.5 2.1 %copy-start.4 = (f32[1,1024,512]{1,2,0:T(8,128)}, f32[1,1024,512]{1,2,0:T(8,128)S(1)}, u32[]{:S(2)}) copy-start(f32[1,1024,512]{1,2,0:T(8,128)S(1)} %convolution_bitcast_fusion.10) | copy-start | bytes 6291460
  30.4 1.3 copy-start.5
  31.8 1.5 copy-start.6
  33.3 109.4 %collective-permute-start.8 = (bf16[384,512]{1,0:T(8,128)(2,1)}, bf16[384,512]{1,0:T(8,128)(2,1)}, u32[]{:S(2)}, u32[]{:S(2)}) collective-permute-start(bf16[384,512]{1,0:T(8,128)(2,1)} %get-tuple-element.24), channel_id=1, source_target_pairs={{0,14},{1,15},{2,0},{3,1},{4,2},{5,3},{6,4},{7,5},{8,6},{9,7},{10,... | collective-permute-start | bytes 1179656 | tf_op jit(solution)/shard_map/ppermute | solution.py:15
  35.1 117.4 %collective-permute-start.11 = (bf16[384,512]{1,0:T(8,128)(2,1)}, bf16[384,512]{1,0:T(8,128)(2,1)}, u32[]{:S(2)}, u32[]{:S(2)}) collective-permute-start(bf16[384,512]{1,0:T(8,128)(2,1)} %get-tuple-element.25), channel_id=1, source_target_pairs={{0,13},{1,14},{2,15},{3,0},{4,1},{5,2},{6,3},{7,4},{8,5},{9,6},{10... | collective-permute-start | bytes 1179656 | tf_op jit(solution)/shard_map/ppermute | solution.py:15
  36.5 0.6 copy-start.20
  37.1 56.4 %collective-permute-start.2 = (bf16[384,512]{1,0:T(8,128)(2,1)}, bf16[384,512]{1,0:T(8,128)(2,1)S(1)}, u32[]{:S(2)}, u32[]{:S(2)}) collective-permute-start(bf16[384,512]{1,0:T(8,128)(2,1)} %get-tuple-element.29), channel_id=1, source_target_pairs={{0,15},{1,0},{2,1},{3,2},{4,3},{5,4},{6,5},{7,6},{8,7},{9,8},{10,9... | collective-permute-start | bytes 1179656 | tf_op jit(solution)/shard_map/ppermute | solution.py:15
  87.5 6.0 %copy-start.15 = (bf16[384,512]{1,0:T(8,128)(2,1)S(1)}, bf16[384,512]{1,0:T(8,128)(2,1)}, u32[]{:S(2)}) copy-start(bf16[384,512]{1,0:T(8,128)(2,1)} %get-tuple-element.26) | copy-start | bytes 1179652
  93.5 7.3 %collective-permute-start.1 = (bf16[384,512]{1,0:T(8,128)(2,1)S(1)}, bf16[384,512]{1,0:T(8,128)(2,1)S(1)}, u32[]{:S(2)}, u32[]{:S(2)}) collective-permute-start(bf16[384,512]{1,0:T(8,128)(2,1)S(1)} %copy-done.15), channel_id=1, source_target_pairs={{0,15},{1,0},{2,1},{3,2},{4,3},{5,4},{6,5},{7,6},{8,7},{9,8},{10,9... | collective-permute-start | bytes 1179656 | tf_op jit(solution)/shard_map/ppermute | solution.py:15
  94.4 10.9 %copy-start.19 = (f32[384]{0:T(512)S(1)}, f32[384]{0:T(512)}, u32[]{:S(2)}) copy-start(f32[384]{0:T(512)} %convert_element_type.158) | copy-start | bytes 4612
  100.8 29.9 %collective-permute-start.6 = (bf16[384,512]{1,0:T(8,128)(2,1)}, bf16[384,512]{1,0:T(8,128)(2,1)}, u32[]{:S(2)}, u32[]{:S(2)}) collective-permute-start(bf16[384,512]{1,0:T(8,128)(2,1)} %get-tuple-element.27), channel_id=1, source_target_pairs={{0,14},{1,15},{2,0},{3,1},{4,2},{5,3},{6,4},{7,5},{8,6},{9,7},{10,... | collective-permute-start | bytes 1179656 | tf_op jit(solution)/shard_map/ppermute | solution.py:15
  113.9 1.7 copy-start.8
  113.9 8.8 %collective-permute-start.7 = (bf16[384,512]{1,0:T(8,128)(2,1)}, bf16[384,512]{1,0:T(8,128)(2,1)S(1)}, u32[]{:S(2)}, u32[]{:S(2)}) collective-permute-start(bf16[384,512]{1,0:T(8,128)(2,1)} %get-tuple-element.30), channel_id=1, source_target_pairs={{0,14},{1,15},{2,0},{3,1},{4,2},{5,3},{6,4},{7,5},{8,6},{9,7},{10,... | collective-permute-start | bytes 1179656 | tf_op jit(solution)/shard_map/ppermute | solution.py:15
  122.7 0.7 copy-start.13
  123.4 5.4 %copy-start.14 = (bf16[384,512]{1,0:T(8,128)(2,1)S(1)}, bf16[384,512]{1,0:T(8,128)(2,1)}, u32[]{:S(2)}) copy-start(bf16[384,512]{1,0:T(8,128)(2,1)} %copy-done.13) | copy-start | bytes 1179652
  123.5 27.8 %collective-permute-start.12 = (bf16[384,512]{1,0:T(8,128)(2,1)}, bf16[384,512]{1,0:T(8,128)(2,1)S(1)}, u32[]{:S(2)}, u32[]{:S(2)}) collective-permute-start(bf16[384,512]{1,0:T(8,128)(2,1)} %get-tuple-element.28), channel_id=1, source_target_pairs={{0,13},{1,14},{2,15},{3,0},{4,1},{5,2},{6,3},{7,4},{8,5},{9,6},{10... | collective-permute-start | bytes 1179656 | tf_op jit(solution)/shard_map/ppermute | solution.py:15
  126.7 5.3 %copy-start = (bf16[3,1024,512]{1,2,0:T(8,128)(2,1)S(1)}, bf16[3,1024,512]{1,2,0:T(8,128)(2,1)}, u32[]{:S(2)}) copy-start(bf16[3,1024,512]{1,2,0:T(8,128)(2,1)} %get-tuple-element.18) | copy-start | bytes 9437188
  128.8 3.3 %copy-start.18 = (f32[384]{0:T(512)S(1)}, f32[384]{0:T(512)}, u32[]{:S(2)}) copy-start(f32[384]{0:T(512)} %convert_element_type.168) | copy-start | bytes 4612
  130.7 45.0 %collective-permute-start.4 = (bf16[384,512]{1,0:T(8,128)(2,1)}, bf16[384,512]{1,0:T(8,128)(2,1)}, u32[]{:S(2)}, u32[]{:S(2)}) collective-permute-start(bf16[384,512]{1,0:T(8,128)(2,1)} %convolution_convert_fusion.2), channel_id=1, source_target_pairs={{0,1},{1,2},{2,3},{3,4},{4,5},{5,6},{6,7},{7,8},{8,9},{9,10},{10,1... | collective-permute-start | bytes 1179656 | tf_op jit(solution)/shard_map/ppermute | solution.py:15
  142.7 1.7 copy-start.9
  147.1 4.1 %copy-start.1 = (bf16[3,1024,512]{1,2,0:T(8,128)(2,1)S(1)}, bf16[3,1024,512]{1,2,0:T(8,128)(2,1)}, u32[]{:S(2)}) copy-start(bf16[3,1024,512]{1,2,0:T(8,128)(2,1)} %get-tuple-element.16) | copy-start | bytes 9437188
  151.3 24.4 %collective-permute-start.9 = (bf16[384,512]{1,0:T(8,128)(2,1)}, bf16[384,512]{1,0:T(8,128)(2,1)}, u32[]{:S(2)}, u32[]{:S(2)}) collective-permute-start(bf16[384,512]{1,0:T(8,128)(2,1)} %convolution_convert_fusion.1), channel_id=1, source_target_pairs={{0,2},{1,3},{2,4},{3,5},{4,6},{5,7},{6,8},{7,9},{8,10},{9,11},{10,... | collective-permute-start | bytes 1179656 | tf_op jit(solution)/shard_map/ppermute | solution.py:15
  151.9 0.7 copy-start.17
  161.0 4.2 %copy-start.10 = (bf16[3,1024,512]{1,2,0:T(8,128)(2,1)}, bf16[3,1024,512]{1,2,0:T(8,128)(2,1)S(1)}, u32[]{:S(2)}) copy-start(bf16[3,1024,512]{1,2,0:T(8,128)(2,1)S(1)} %multiply_convert_fusion) | copy-start | bytes 9437188
  167.9 4.2 %copy-start.7 = (bf16[3,1024,512]{1,2,0:T(8,128)(2,1)S(1)}, bf16[3,1024,512]{1,2,0:T(8,128)(2,1)}, u32[]{:S(2)}) copy-start(bf16[3,1024,512]{1,2,0:T(8,128)(2,1)} %get-tuple-element.21) | copy-start | bytes 9437188
  172.1 13.7 %collective-permute-start.14 = (bf16[384,512]{1,0:T(8,128)(2,1)}, bf16[384,512]{1,0:T(8,128)(2,1)S(1)}, u32[]{:S(2)}, u32[]{:S(2)}) collective-permute-start(bf16[384,512]{1,0:T(8,128)(2,1)} %convolution_convert_fusion), channel_id=1, source_target_pairs={{0,3},{1,4},{2,5},{3,6},{4,7},{5,8},{6,9},{7,10},{8,11},{9,12},{10... | collective-permute-start | bytes 1179656 | tf_op jit(solution)/shard_map/ppermute | solution.py:15
Sparse Core Ops, SparseCore 0:
  9.5 74.7 all-gather.1
where the time goes:
time: 196 us; the launch traced here: 195 us
  waiting for transfers between devices  63 us (32%)
  matrix products  53.6 us (27%)
  other arithmetic  25.6 us (13%)
  local copies, waits for them, and re-layouts  19.8 us (10%)
  starting transfers between devices  19.4 us (10%)
  between operations  13.9 us (7%)
    all_gather x1, waiting for transfers between devices, body(): whole_initial = lax.all_gather(initial_fast, 'seq', axis=1, tiled=True)  46 us
    dot_general x16, matrix products, contract_last(): lax.dot_general(left_side, right_side, (((1,), (1,)), ((), ())), preferre...  24.2 us
    ppermute x15, starting transfers between devices, shifted(): return lax.ppermute(value, axis, pairs)  19.4 us
    ppermute x15, waiting for transfers between devices, shifted(): return lax.ppermute(value, axis, pairs)  16.3 us
    dot_general x4, matrix products, serve_queries(): jnp.dot(hidden, fast[2], preferred_element_type=jnp.float32)  15.8 us
    dot_general x12, matrix products, contract_first(): lax.dot_general(left_side, right_side, (((0,), (0,)), ((), ())), preferre...  13.5 us
    select_n x3, other arithmetic, body(): carried = jnp.where(restart, whole_initial, advanced)  13.2 us
    unnamed x43, local copies, waits for them, and re-layouts  9.12 us
  transfers between devices with their start and end apart: 16, of which 4 were waited for; matrix products, arithmetic and copies ran while one was open for 46% of the time, Pallas kernels for 0%

commit v1 on v0

v1 whole, which is shorter than its diff:
```python
import functools

import jax
import jax.numpy as jnp
from jax import lax
from jax.experimental import pallas as pl
from jax.experimental.pallas import tpu as pltpu
from jax.sharding import PartitionSpec as P

epsilon = 1e-06
AXIS = "seq"


def contract_last(left_side, right_side):
    return lax.dot_general(
        left_side, right_side, (((1,), (1,)), ((), ())), preferred_element_type=jnp.float32
    )


def plain_dot(left_side, right_side):
    return jnp.dot(left_side, right_side, preferred_element_type=jnp.float32)


def sigmoid(value):
    return 0.5 * jnp.tanh(0.5 * value) + 0.5


def rescale(updated, previous):
    old_square = jnp.sum(previous * previous, axis=-1, keepdims=True) + epsilon
    new_square = jnp.sum(updated * updated, axis=-1, keepdims=True) + epsilon
    return (updated * (jnp.sqrt(old_square) * lax.rsqrt(new_square))).astype(jnp.bfloat16)


def kernel(
    n, ticks, part,
    fast, init, k_in, t_in, q_in, out,
    st, ini, kb, tb, qb, ans, acc,
    local_sem, own_sem, data_send, data_recv, ans_send, ans_recv, init_send, init_recv, fwd_send, fwd_recv,
):
    p = lax.axis_index(AXIS)
    last = n - 1
    reach = ticks - 1
    hid = st.shape[1]

    def local_copies():
        return [
            pltpu.make_async_copy(k_in.at[0, 0], kb.at[0], local_sem.at[0]),
            pltpu.make_async_copy(t_in.at[0], tb.at[0], local_sem.at[1]),
            pltpu.make_async_copy(fast.at[0], st, local_sem.at[2]),
            pltpu.make_async_copy(q_in.at[0, 0], qb.at[0], local_sem.at[3]),
        ]

    def data_copies(t):
        dest = lax.rem(p - t + n, n)
        pairs = [(k_in.at[0, t], kb.at[t]), (t_in.at[t], tb.at[t]), (q_in.at[0, t], qb.at[t])]
        return [
            pltpu.make_async_remote_copy(
                src_ref=src, dst_ref=dst,
                send_sem=data_send.at[t, i], recv_sem=data_recv.at[t, i],
                device_id={AXIS: dest}, device_id_type=pl.DeviceIdType.MESH,
            )
            for i, (src, dst) in enumerate(pairs)
        ]

    def answer_copy(t):
        return pltpu.make_async_remote_copy(
            src_ref=ans.at[t], dst_ref=out.at[0, t],
            send_sem=ans_send.at[t], recv_sem=ans_recv.at[t],
            device_id={AXIS: lax.rem(p + t, n)}, device_id_type=pl.DeviceIdType.MESH,
        )

    def shard_copy(i):
        return pltpu.make_async_remote_copy(
            src_ref=init, dst_ref=ini.at[i],
            send_sem=init_send, recv_sem=init_recv.at[i],
            device_id={AXIS: last}, device_id_type=pl.DeviceIdType.MESH,
        )

    def forward_copy(i):
        return pltpu.make_async_remote_copy(
            src_ref=ini, dst_ref=ini,
            send_sem=fwd_send.at[i], recv_sem=fwd_recv,
            device_id={AXIS: last - i}, device_id_type=pl.DeviceIdType.MESH,
        )

    own_shard = pltpu.make_async_copy(init, ini.at[last], own_sem)

    for copy in local_copies():
        copy.start()

    barrier = pltpu.get_barrier_semaphore()
    for off in range(1, ticks):
        for other in (lax.rem(p + off, n), lax.rem(p - off + n, n)):
            pl.semaphore_signal(
                barrier, inc=1, device_id={AXIS: other}, device_id_type=pl.DeviceIdType.MESH
            )
    far_from, far_to = reach, n - 1 - reach
    far = jnp.logical_and(p >= far_from, p < far_to)

    @pl.when(far)
    def _():
        pl.semaphore_signal(
            barrier, inc=1, device_id={AXIS: last}, device_id_type=pl.DeviceIdType.MESH
        )
        pl.semaphore_wait(barrier, 2 * reach + 1)

    @pl.when(p == last)
    def _():
        @pl.loop(far_from, far_to)
        def _(i):
            pl.semaphore_signal(
                barrier, inc=1, device_id={AXIS: i}, device_id_type=pl.DeviceIdType.MESH
            )

        pl.semaphore_wait(barrier, 2 * reach + (far_to - far_from))

    @pl.when(jnp.logical_and(jnp.logical_not(far), p != last))
    def _():
        pl.semaphore_wait(barrier, 2 * reach)

    for t in range(1, ticks):
        for copy in data_copies(t):
            copy.start()
        if t == 1:
            @pl.when(p == last)
            def _():
                own_shard.start()

            @pl.when(p != last)
            def _():
                shard_copy(p).start()

    for copy in local_copies():
        copy.wait()

    @pl.loop(0, ticks)
    def _(t):
        @pl.when(t > 0)
        def _():
            for copy in data_copies(t):
                copy.wait_recv()

        @pl.when(jnp.logical_and(t > 0, p + t == n))
        def _():
            @pl.when(p == last)
            def _():
                own_shard.wait()

                @pl.loop(0, last)
                def _(i):
                    shard_copy(i).wait_recv()

                for i in range(1, reach):
                    forward_copy(i).start()

            @pl.when(p != last)
            def _():
                forward_copy(1).wait_recv()

            rows = init.shape[1]
            for i in range(n):
                for m in range(3):
                    st[m, pl.ds(i * rows, rows), :] = ini[i, m]

        @pl.loop(0, hid // part)
        def _(c):
            span = pl.ds(pl.multiple_of(c * part, part), part)
            keys, target, asked = kb[t], tb[t], qb[t]
            gate, up, down = st[0, span, :], st[1, span, :], st[2, span, :]
            gate_pre = contract_last(gate, keys)
            up_pre = contract_last(up, keys)
            back_grad = contract_last(down, target)
            sig = sigmoid(gate_pre)
            silu = gate_pre * sig
            hidden = (silu * up_pre).astype(jnp.bfloat16)
            grad_gate = (
                back_grad * up_pre * sig * (1.0 + gate_pre * (1.0 - sig))
            ).astype(jnp.bfloat16)
            grad_up = (back_grad * silu).astype(jnp.bfloat16)
            old_gate = gate.astype(jnp.float32)
            old_up = up.astype(jnp.float32)
            old_down = down.astype(jnp.float32)
            new_gate = rescale(old_gate + plain_dot(grad_gate, keys), old_gate)
            new_up = rescale(old_up + plain_dot(grad_up, keys), old_up)
            new_down = rescale(old_down + plain_dot(hidden, target), old_down)
            st[0, span, :] = new_gate
            st[1, span, :] = new_up
            st[2, span, :] = new_down
            pre = contract_last(asked, new_gate)
            ahead = contract_last(asked, new_up)
            served = (pre * sigmoid(pre) * ahead).astype(jnp.bfloat16)
            term = plain_dot(served, new_down)

            @pl.when(c == 0)
            def _():
                acc[...] = term

            @pl.when(c > 0)
            def _():
                acc[...] += term

        ans[t] = acc[...].astype(jnp.bfloat16)

        @pl.when(t == 0)
        def _():
            pltpu.make_async_copy(ans.at[0], out.at[0, 0], local_sem.at[0]).start()

        @pl.when(t > 0)
        def _():
            answer_copy(t).start()

    pltpu.make_async_copy(ans.at[0], out.at[0, 0], local_sem.at[0]).wait()
    for t in range(1, ticks):
        for copy in data_copies(t):
            copy.wait_send()
        answer_copy(t).wait_send()
        answer_copy(t).wait_recv()

    @pl.when(p == last)
    def _():
        for i in range(1, reach):
            forward_copy(i).wait_send()

    @pl.when(p != last)
    def _():
        shard_copy(p).wait_send()


def body(fast_state, initial_fast, queries, token_keys, token_values, step_sizes):
    n = lax.axis_size(AXIS)
    _, ticks, span, width = queries.shape
    hid = fast_state.shape[2]
    target = (
        step_sizes[0].astype(jnp.float32)[:, :, None] * token_values[0].astype(jnp.float32)
    ).astype(jnp.bfloat16)
    slots = pltpu.VMEM((ticks, span, width), jnp.bfloat16)
    dma = pltpu.SemaphoreType.DMA
    anywhere = pl.BlockSpec(memory_space=pl.ANY)
    return pl.pallas_call(
        functools.partial(kernel, n, ticks, 256),
        out_shape=jax.ShapeDtypeStruct(queries.shape, jnp.bfloat16),
        in_specs=[anywhere] * 5,
        out_specs=anywhere,
        scratch_shapes=[
            pltpu.VMEM(fast_state.shape[1:], jnp.bfloat16),
            pltpu.VMEM((n,) + initial_fast.shape, jnp.bfloat16),
            slots, slots, slots, slots,
            pltpu.VMEM((span, width), jnp.float32),
            dma((4,)), dma, dma((ticks, 3)), dma((ticks, 3)), dma((ticks,)), dma((ticks,)),
            dma, dma((n,)), dma((ticks,)), dma,
        ],
        compiler_params=pltpu.CompilerParams(
            collective_id=0, has_side_effects=True, vmem_limit_bytes=48 * 1024 * 1024
        ),
        cost_estimate=pl.CostEstimate(
            flops=18 * ticks * span * width * hid,
            bytes_accessed=16 * 1024 * 1024,
            transcendentals=2 * ticks * span * hid,
        ),
    )(fast_state, initial_fast, token_keys, target, queries)


def solution(mesh):
    return jax.shard_map(
        body,
        mesh=mesh,
        in_specs=(
            P(("grp", AXIS), None, None, None),
            P(None, AXIS, None),
            P(("grp", AXIS), None, None, None),
            P(("grp", AXIS), None, None, None),
            P(("grp", AXIS), None, None, None),
            P(("grp", AXIS), None, None),
        ),
        out_specs=P(("grp", AXIS), None, None, None),
        check_vma=False,
    )
```

time: 196 us -> 138 us (0.70)
  the two profiles are of different devices: /device:TPU:1 before, /device:TPU:0 now
where the time goes in v1:
time: 138 us
  Pallas kernels  134 us (97%)
  other arithmetic  2.6 us (2%)
    pallas_call x1, Pallas kernels, body(): pl.pallas_call(functools.partial(kernel, n, ticks, 256), out_shape=jax.Sh...  134 us

profile of v1, /device:TPU:0, one launch (start us, length us, event | category | flops | bytes accessed | tf_op | source)
XLA Modules:
  0.0 137.5 jit_solution(16373600401323477763)
XLA Ops:
  0.0 0.7 bitcast_convert_fusion
  0.7 0.0 copy-start
  0.7 0.0 copy-start.1
  0.7 1.9 %fusion.t_in = bf16[4,384,512]{2,1,0:T(8,128)(2,1)S(1)} fusion(bf16[1,4,384,512]{3,2,1,0:T(8,128)(2,1)} %param.10, f32[4,384]{1,0:T(4,128)S(1)} %bitcast_convert_fusion), kind=kLoop, calls=%fused_computation.1 | loop fusion | flops 2359296 | bytes 3151872 | tf_op jit(solution)/shard_map/convert_element_type | solution.py:235
  2.6 0.0 copy-done
  2.6 0.0 copy-done.1
  2.6 133.7 %shard_map.64 = bf16[1,4,384,512]{3,2,1,0:T(8,128)(2,1)S(1)} custom-call(bf16[1,3,1024,512]{3,2,1,0:T(8,128)(2,1)} %fast.1, bf16[3,64,512]{2,1,0:T(8,128)(2,1)S(1)} %copy-done.1, bf16[1,4,384,512]{3,2,1,0:T(8,128)(2,1)S(1)} %copy-done, bf16[4,384,512]{2,1,0:T(8,128)(2,1)S(1)} %fusion.t_in, bf16[1,4,384,512]{3,2,1,0:T(8,128)(2,1)} %q_in.1), custom_call_target="tpu_custom_call" | custom-call | flops 14495514624 | bytes 16777216 | tf_op jit(solution)/shard_map/pallas_call | solution.py:239
  136.4 1.1 copy.8
Async XLA Ops:
  0.7 1.9 %copy-start = (bf16[1,4,384,512]{3,2,1,0:T(8,128)(2,1)S(1)}, bf16[1,4,384,512]{3,2,1,0:T(8,128)(2,1)}, u32[]{:S(2)}) copy-start(bf16[1,4,384,512]{3,2,1,0:T(8,128)(2,1)} %k_in.1) | copy-start | bytes 4718596
  0.7 1.9 %copy-start.1 = (bf16[3,64,512]{2,1,0:T(8,128)(2,1)S(1)}, bf16[3,64,512]{2,1,0:T(8,128)(2,1)}, u32[]{:S(2)}) copy-start(bf16[3,64,512]{2,1,0:T(8,128)(2,1)} %init.1) | copy-start | bytes 589828

commit v2 on v1

v2 whole, which is shorter than its diff:
```python
import functools

import jax
import jax.numpy as jnp
from jax import lax
from jax.experimental import pallas as pl
from jax.experimental.pallas import tpu as pltpu
from jax.sharding import PartitionSpec as P

epsilon = 1e-06
AXIS = "seq"


def contract_last(left_side, right_side):
    return lax.dot_general(
        left_side, right_side, (((1,), (1,)), ((), ())), preferred_element_type=jnp.float32
    )


def plain_dot(left_side, right_side):
    return jnp.dot(left_side, right_side, preferred_element_type=jnp.float32)


def sigmoid(value):
    return 0.5 * jnp.tanh(0.5 * value) + 0.5


def rescale(updated, previous):
    old_square = jnp.sum(previous * previous, axis=-1, keepdims=True) + epsilon
    new_square = jnp.sum(updated * updated, axis=-1, keepdims=True) + epsilon
    return (updated * (jnp.sqrt(old_square) * lax.rsqrt(new_square))).astype(jnp.bfloat16)


def restarts(ticks):
    units = []
    filled = [ticks - 1, ticks - 1]
    for late in range(1, ticks):
        device = 0 if late == 1 else 1
        for tick in range(late, ticks):
            units.append((device, filled[device], tick - late, tick, tick == late))
            filled[device] += 1
    return units, max(filled)


def kernel(
    n, ticks, part,
    fast, init, k_in, t_in, q_in, out,
    st, ini, kb, tb, qb, ans, acc,
    local_sem, own_sem, data_send, data_recv, ans_send, ans_recv, init_send, init_recv, fwd_send, fwd_recv,
):
    p = lax.axis_index(AXIS)
    reach = ticks - 1
    hid = st.shape[2]
    extra, final = restarts(ticks)
    slot_of = list(range(reach)) + [final]

    def local_copies():
        return [
            pltpu.make_async_copy(k_in.at[0, 0], kb.at[0], local_sem.at[0]),
            pltpu.make_async_copy(t_in.at[0], tb.at[0], local_sem.at[1]),
            pltpu.make_async_copy(fast.at[0], st.at[0], local_sem.at[2]),
            pltpu.make_async_copy(q_in.at[0, 0], qb.at[0], local_sem.at[3]),
        ]

    def pairs(t, slot):
        return [
            (k_in.at[0, t], kb.at[slot]), (t_in.at[t], tb.at[slot]), (q_in.at[0, t], qb.at[slot])
        ]

    def remote(src, dst, send, recv, dest):
        return pltpu.make_async_remote_copy(
            src_ref=src, dst_ref=dst, send_sem=send, recv_sem=recv,
            device_id={AXIS: dest}, device_id_type=pl.DeviceIdType.MESH,
        )

    def data_copies(t, slot, dest):
        return [
            remote(src, dst, data_send.at[t, i], data_recv.at[slot, i], dest)
            for i, (src, dst) in enumerate(pairs(t, slot))
        ]

    def own_copies(t, slot):
        return [
            pltpu.make_async_copy(src, dst, data_recv.at[slot, i])
            for i, (src, dst) in enumerate(pairs(t, slot))
        ]

    def answer_copy(slot, t, home):
        return remote(ans.at[slot], out.at[0, t], ans_send.at[slot], ans_recv.at[t], home)

    def own_answer(slot, t):
        return pltpu.make_async_copy(ans.at[slot], out.at[0, t], ans_recv.at[t])

    def shard_copy(i):
        return remote(init, ini.at[i], init_send, init_recv.at[i], 0)

    def forward_copy():
        return remote(ini, ini, fwd_send, fwd_recv, 1)

    def signal(other):
        pl.semaphore_signal(
            barrier, inc=1, device_id={AXIS: other}, device_id_type=pl.DeviceIdType.MESH
        )

    own_shard = pltpu.make_async_copy(init, ini.at[0], own_sem)

    for copy in local_copies():
        copy.start()

    barrier = pltpu.get_barrier_semaphore()
    for off in range(1, ticks):
        @pl.when(p + off < n)
        def _():
            signal(p + off)

        @pl.when(p >= off)
        def _():
            signal(p - off)

    @pl.when(p > reach)
    def _():
        signal(0)

    @pl.when(p == 0)
    def _():
        @pl.loop(ticks, n)
        def _(i):
            signal(i)

        pl.semaphore_wait(barrier, n - 1)

    for off in range(1, ticks):
        @pl.when(p == off)
        def _():
            pl.semaphore_wait(barrier, off + min(reach, n - 1 - off))

        @pl.when(p == n - off)
        def _():
            pl.semaphore_wait(barrier, reach + off)

    @pl.when(jnp.logical_and(p > reach, p < n - reach))
    def _():
        pl.semaphore_wait(barrier, 2 * reach + 1)

    @pl.when(p == 0)
    def _():
        own_shard.start()

    @pl.when(p > 0)
    def _():
        shard_copy(p).start()

    for t in range(1, ticks):
        @pl.when(p >= t)
        def _():
            for copy in data_copies(t, slot_of[t], p - t):
                copy.start()

        for device, slot, section, tick, _fresh in extra:
            if tick == t:
                @pl.when(p == section)
                def _():
                    moves = (
                        own_copies(t, slot) if device == section else data_copies(t, slot, device)
                    )
                    for copy in moves:
                        copy.start()


    for copy in local_copies():
        copy.wait()

    def unpack():
        rows = init.shape[1]
        for i in range(n):
            for m in range(3):
                st[1, m, pl.ds(i * rows, rows), :] = ini[i, m]

    def run(step):
        which = lax.rem(step // reach, 2)

        @pl.when(step > 0)
        def _():
            for copy in own_copies(1, step):
                copy.wait()

        @pl.when(jnp.logical_and(step == reach, p == 0))
        def _():
            own_shard.wait()

            @pl.loop(1, n)
            def _(i):
                shard_copy(i).wait_recv()

            forward_copy().start()

        @pl.when(jnp.logical_and(step == reach, p == 1))
        def _():
            forward_copy().wait_recv()

        for device, slot, _section, _tick, fresh in extra:
            if fresh:
                @pl.when(jnp.logical_and(step == slot, p == device))
                def _():
                    unpack()

        @pl.loop(0, hid // part, unroll=True)
        def _(c):
            span = pl.ds(pl.multiple_of(c * part, part), part)
            keys, target, asked = kb[step], tb[step], qb[step]
            gate, up, down = st[which, 0, span, :], st[which, 1, span, :], st[which, 2, span, :]
            gate_pre = contract_last(gate, keys)
            up_pre = contract_last(up, keys)
            back_grad = contract_last(down, target)
            sig = sigmoid(gate_pre)
            silu = gate_pre * sig
            hidden = (silu * up_pre).astype(jnp.bfloat16)
            grad_gate = (
                back_grad * up_pre * sig * (1.0 + gate_pre * (1.0 - sig))
            ).astype(jnp.bfloat16)
            grad_up = (back_grad * silu).astype(jnp.bfloat16)
            old_gate = gate.astype(jnp.float32)
            old_up = up.astype(jnp.float32)
            old_down = down.astype(jnp.float32)
            new_gate = rescale(old_gate + plain_dot(grad_gate, keys), old_gate)
            new_up = rescale(old_up + plain_dot(grad_up, keys), old_up)
            new_down = rescale(old_down + plain_dot(hidden, target), old_down)
            st[which, 0, span, :] = new_gate
            st[which, 1, span, :] = new_up
            st[which, 2, span, :] = new_down
            pre = contract_last(asked, new_gate)
            ahead = contract_last(asked, new_up)
            served = (pre * sigmoid(pre) * ahead).astype(jnp.bfloat16)
            term = plain_dot(served, new_down)

            @pl.when(c == 0)
            def _():
                acc[...] = term

            @pl.when(c > 0)
            def _():
                acc[...] += term

        ans[step] = acc[...].astype(jnp.bfloat16)

        @pl.when(step == 0)
        def _():
            own_answer(0, 0).start()

        for t in range(1, ticks):
            @pl.when(step == slot_of[t])
            def _():
                answer_copy(slot_of[t], t, p + t).start()

        for device, slot, section, tick, _fresh in extra:
            @pl.when(jnp.logical_and(step == slot, p == device))
            def _():
                if device == section:
                    own_answer(slot, tick).start()
                else:
                    answer_copy(slot, tick, section).start()

    @pl.loop(0, final + 1)
    def _(step):
        middle = jnp.logical_and(step >= reach, step < final)
        tick = step - (step // final) * (final - reach)
        chain = jnp.logical_and(jnp.logical_not(middle), p + tick < n)

        @pl.when(jnp.logical_or(chain, jnp.logical_and(middle, p < 2)))
        def _():
            run(step)

    for t in range(ticks):
        own_answer(0, t).wait()
    for t in range(1, ticks):
        @pl.when(p >= t)
        def _():
            for copy in data_copies(t, slot_of[t], p - t):
                copy.wait_send()

        @pl.when(p + t < n)
        def _():
            answer_copy(slot_of[t], t, p + t).wait_send()

    for device, slot, section, tick, _fresh in extra:
        if device != section:
            @pl.when(p == section)
            def _():
                for copy in data_copies(tick, slot, device):
                    copy.wait_send()

            @pl.when(p == device)
            def _():
                answer_copy(slot, tick, section).wait_send()

    @pl.when(p == 0)
    def _():
        forward_copy().wait_send()

    @pl.when(p > 0)
    def _():
        shard_copy(p).wait_send()


def body(fast_state, initial_fast, queries, token_keys, token_values, step_sizes):
    n = lax.axis_size(AXIS)
    _, ticks, span, width = queries.shape
    hid = fast_state.shape[2]
    target = (
        step_sizes[0].astype(jnp.float32)[:, :, None] * token_values[0].astype(jnp.float32)
    ).astype(jnp.bfloat16)
    held = restarts(ticks)[1] + 1
    slots = pltpu.VMEM((held, span, width), jnp.bfloat16)
    dma = pltpu.SemaphoreType.DMA
    anywhere = pl.BlockSpec(memory_space=pl.ANY)
    return pl.pallas_call(
        functools.partial(kernel, n, ticks, 256),
        out_shape=jax.ShapeDtypeStruct(queries.shape, jnp.bfloat16),
        in_specs=[anywhere] * 5,
        out_specs=anywhere,
        scratch_shapes=[
            pltpu.VMEM((2,) + fast_state.shape[1:], jnp.bfloat16),
            pltpu.VMEM((n,) + initial_fast.shape, jnp.bfloat16),
            slots, slots, slots, slots,
            pltpu.VMEM((span, width), jnp.float32),
            dma((4,)), dma, dma((ticks, 3)), dma((held, 3)), dma((held,)), dma((ticks,)),
            dma, dma((n,)), dma, dma,
        ],
        compiler_params=pltpu.CompilerParams(
            collective_id=0, has_side_effects=True, vmem_limit_bytes=48 * 1024 * 1024
        ),
        cost_estimate=pl.CostEstimate(
            flops=18 * ticks * span * width * hid,
            bytes_accessed=16 * 1024 * 1024,
            transcendentals=2 * ticks * span * hid,
        ),
    )(fast_state, initial_fast, token_keys, target, queries)


def solution(mesh):
    return jax.shard_map(
        body,
        mesh=mesh,
        in_specs=(
            P(("grp", AXIS), None, None, None),
            P(None, AXIS, None),
            P(("grp", AXIS), None, None, None),
            P(("grp", AXIS), None, None, None),
            P(("grp", AXIS), None, None, None),
            P(("grp", AXIS), None, None),
        ),
        out_specs=P(("grp", AXIS), None, None, None),
        check_vma=False,
    )
```

time: 138 us -> 120 us (0.87)
  the two profiles are of different devices: /device:TPU:0 before, /device:TPU:1 now
where the time goes in v2:
time: 120 us
  Pallas kernels  116 us (97%)
  other arithmetic  2.6 us (2%)
    pallas_call x1, Pallas kernels, body(): pl.pallas_call(functools.partial(kernel, n, ticks, 256), out_shape=jax.Sh...  116 us

profile of v2, /device:TPU:1, one launch (start us, length us, event | category | flops | bytes accessed | tf_op | source)
XLA Modules:
  0.0 119.5 jit_solution(17044470030358193109)
XLA Ops:
  0.0 0.7 bitcast_convert_fusion
  0.7 0.0 copy-start
  0.7 0.0 copy-start.1
  0.7 1.9 %fusion.t_in = bf16[4,384,512]{2,1,0:T(8,128)(2,1)S(1)} fusion(bf16[1,4,384,512]{3,2,1,0:T(8,128)(2,1)} %param.10, f32[4,384]{1,0:T(4,128)S(1)} %bitcast_convert_fusion), kind=kLoop, calls=%fused_computation.1 | loop fusion | flops 2359296 | bytes 3151872 | tf_op jit(solution)/shard_map/convert_element_type | solution.py:311
  2.6 0.0 copy-done
  2.6 0.0 copy-done.1
  2.6 115.7 %shard_map.64 = bf16[1,4,384,512]{3,2,1,0:T(8,128)(2,1)S(1)} custom-call(bf16[1,3,1024,512]{3,2,1,0:T(8,128)(2,1)} %fast.1, bf16[3,64,512]{2,1,0:T(8,128)(2,1)S(1)} %copy-done.1, bf16[1,4,384,512]{3,2,1,0:T(8,128)(2,1)S(1)} %copy-done, bf16[4,384,512]{2,1,0:T(8,128)(2,1)S(1)} %fusion.t_in, bf16[1,4,384,512]{3,2,1,0:T(8,128)(2,1)} %q_in.1), custom_call_target="tpu_custom_call" | custom-call | flops 14495514624 | bytes 16777216 | tf_op jit(solution)/shard_map/pallas_call | solution.py:316
  118.4 1.1 copy.8
Async XLA Ops:
  0.7 1.9 %copy-start = (bf16[1,4,384,512]{3,2,1,0:T(8,128)(2,1)S(1)}, bf16[1,4,384,512]{3,2,1,0:T(8,128)(2,1)}, u32[]{:S(2)}) copy-start(bf16[1,4,384,512]{3,2,1,0:T(8,128)(2,1)} %k_in.1) | copy-start | bytes 4718596
  0.7 1.9 %copy-start.1 = (bf16[3,64,512]{2,1,0:T(8,128)(2,1)S(1)}, bf16[3,64,512]{2,1,0:T(8,128)(2,1)}, u32[]{:S(2)}) copy-start(bf16[3,64,512]{2,1,0:T(8,128)(2,1)} %init.1) | copy-start | bytes 589828
